TPU v7x, 128 devices: a whole 4x4x4 slice. The times are simulated.
128 devices in a mesh: pairs: 4 (over z), virt: 32 (over x, y, core).
Axes of the slice: x: 4, y: 4, z: 4, core: 2. Of those that a mesh axis runs over, the one named last changes fastest.
Arguments:
- amps: bfloat16 [32, 512, 64, 256], P('virt', 'pairs'), may hold values from -6 to 6
- fock: bfloat16 [2048, 2048], P(('pairs', 'virt')), may hold values from -0.375 to 0.375
- cols: int32 [32, 512, 4], P(None, 'pairs'), may hold values from 0 to 31, all different within a row; in each aligned block of 128 rows (0 to 127, 128 to 255, ..., all dimensions but the last counted through in order) at most 32 rows name the same one
Outputs:
- residual: float32 [32, 512, 64, 256], P('virt', 'pairs')
Inputs may be any that keep to these rules, and one draw needn't show every extreme that they name: `cols`: within one row tile and one aligned block of 128 pair rows, no column tile is named by more than 32 rows, and some column tile is named by exactly 32; the 4 numbers of one row differ.
All inputs are finite; a program needn't handle non-finite values.
Results may differ from a plain program's by a relative error of at most 0.0021.
Values may be sent and summed in bfloat16 or wider, within the bound.
A program may use at most 256 MiB of HBM per device.

v0:
```python
import math

import jax
import jax.numpy as jnp
from jax import lax
from jax.sharding import PartitionSpec as P

MOST = 32


def dress_tiles(tile_rows, col_list, targets, fock_tiles, out_form):
    count = tile_rows.shape[0]
    kept_count = col_list.shape[1]
    tile_size = fock_tiles.shape[1]
    chosen = fock_tiles[targets[:, :, None], :, col_list[:, None, :], :]
    split_rows = tile_rows.reshape(count, tile_size, kept_count, tile_size)
    return jnp.einsum(
        "mxkc,mjkyc->" + out_form, split_rows, chosen, preferred_element_type=jnp.float32
    )


def blockwise(func, arrays, block_size):
    whole = arrays[0].shape[0]
    step_size = math.gcd(whole, block_size)
    shaped = tuple(
        (item.reshape((whole // step_size, step_size) + item.shape[1:]) for item in arrays)
    )
    result = lax.map(lambda parts: func(*parts), shaped)
    return result.reshape((whole,) + result.shape[2:])


def per_device(amps, fock, cols):
    tiles_dev = amps.shape[0]
    rows_dev = amps.shape[1]
    tile_size = amps.shape[2]
    kept_count = cols.shape[2]
    ntiles = cols.shape[0]
    nvirt = lax.axis_size("virt")
    virt_index = lax.axis_index("virt")
    full_fock = lax.all_gather(fock, ("pairs", "virt"), axis=0, tiled=True)
    fock_tiles = full_fock.reshape(ntiles, tile_size, ntiles, tile_size)
    my_cols = lax.dynamic_slice_in_dim(cols, virt_index * tiles_dev, tiles_dev, 0)
    entries = tiles_dev * rows_dev * kept_count

    def own_block(tile_rows, col_list):
        return dress_tiles(tile_rows, col_list, col_list, fock_tiles, "mjxy")

    own_part = blockwise(
        own_block,
        (
            amps.reshape(tiles_dev * rows_dev, tile_size, kept_count * tile_size),
            my_cols.reshape(tiles_dev * rows_dev, kept_count),
        ),
        256,
    )
    capacity = tiles_dev * tiles_dev * MOST
    flat_owner = (cols // tiles_dev).reshape(nvirt, entries)
    held_here = flat_owner == virt_index
    slot_rank = jnp.cumsum(held_here.astype(jnp.int32), axis=1) - 1
    slot_index = jnp.where(held_here, slot_rank, capacity)
    positions = jnp.broadcast_to(jnp.arange(entries, dtype=jnp.int32)[None, :], (nvirt, entries))
    peer_rows = jnp.broadcast_to(jnp.arange(nvirt, dtype=jnp.int32)[:, None], (nvirt, entries))
    slot_entry = (
        jnp.zeros((nvirt, capacity + 1), jnp.int32)
        .at[peer_rows, slot_index]
        .set(positions)[:, :capacity]
    )
    slot_live = (
        jnp.zeros((nvirt, capacity + 1), jnp.float32)
        .at[peer_rows, slot_index]
        .set(1.0)[:, :capacity]
    )
    tile_part = slot_entry // (rows_dev * kept_count)
    row_part = slot_entry // kept_count % rows_dev
    kept_part = slot_entry % kept_count
    dest_tiles = jnp.arange(nvirt, dtype=jnp.int32)[:, None] * tiles_dev + tile_part
    target_tile = cols[dest_tiles, row_part, kept_part]
    local_tile = jnp.clip(target_tile - virt_index * tiles_dev, 0, tiles_dev - 1)
    mirror_row = rows_dev - 1 - row_part
    mirror_cols = cols[target_tile, mirror_row]

    def mirror_block(tile_index, row_index, col_list, targets):
        tile_rows = amps[tile_index, row_index]
        return dress_tiles(tile_rows, col_list, targets[:, None], fock_tiles, "mjyx")[:, 0]

    slots = nvirt * capacity
    mirrored = blockwise(
        mirror_block,
        (
            local_tile.reshape(slots),
            mirror_row.reshape(slots),
            mirror_cols.reshape(slots, kept_count),
            dest_tiles.reshape(slots),
        ),
        256,
    )
    outgoing = (mirrored * slot_live.reshape(slots)[:, None, None]).astype(jnp.bfloat16)
    outgoing = outgoing.reshape(nvirt, capacity, tile_size, tile_size)
    received = lax.all_to_all(outgoing, "virt", split_axis=0, concat_axis=0, tiled=True)
    source_tile = my_cols.reshape(entries) // tiles_dev
    source_match = (source_tile[:, None] == jnp.arange(nvirt, dtype=jnp.int32)[None, :]).astype(
        jnp.int32
    )
    arrival = jnp.cumsum(source_match, axis=0) - 1
    arrival_slot = jnp.sum(arrival * source_match, axis=1)
    returned = received[source_tile, arrival_slot]
    combined = own_part.reshape(entries, tile_size, tile_size) + returned.astype(jnp.float32)
    combined = combined.reshape(tiles_dev, rows_dev, kept_count, tile_size, tile_size)
    return jnp.transpose(combined, (0, 1, 3, 2, 4)).reshape(
        tiles_dev, rows_dev, tile_size, kept_count * tile_size
    )


def solution(mesh):
    in_specs = (P("virt", "pairs", None, None), P(("pairs", "virt"), None), P(None, "pairs", None))
    out_specs = P("virt", "pairs", None, None)
    return jax.shard_map(
        per_device, mesh=mesh, in_specs=in_specs, out_specs=out_specs, check_vma=False
    )
```

profile of v0, /device:TPU:72, one launch (start us, length us, event | category | flops | bytes accessed | tf_op | source)
XLA Modules:
  0.0 820.0 jit_solution(4367933427332588995)
XLA Ops:
  6.5 0.7 all-gather.2.cloned.1.call-update
  7.3 1.5 copy.145
  8.8 0.9 fusion.41
  9.9 1.2 reduce-window.14
  11.9 0.7 multiply_reduce_fusion
  12.8 0.8 and_reduce_fusion
  13.9 60.3 %scatter_custom_fusion = s32[1056]{0:T(1024)S(1)} fusion(s32[16384]{0:T(1024)S(1)} %bitcast.128, s32[16384]{0:T(1024)S(1)} %bitcast.130, s32[]{:T(128)} %constant.132.clone.1), kind=kCustom, calls=%fused_computation.89 | custom fusion | bytes 4228
  74.5 9.7 %gather_fusion.3 = s32[1024]{0:T(1024)S(1)} fusion(s32[32,128,4]{1,2,0:T(4,128)S(1)} %copy-done, s32[1024]{0:T(1024)S(1)} %reshape.397), kind=kCustom, calls=%fused_computation.3 | custom fusion | bytes 20480 | tf_op jit(solution)/shard_map/gather | solution.py:77
  84.4 6.8 gather_fusion.4
  91.6 60.5 %scatter_custom_fusion.1 = f32[1056]{0:T(1024)S(1)} fusion(s32[16384]{0:T(1024)S(1)} %bitcast.129, f32[16384]{0:T(1024)S(1)} %broadcast.431, f32[]{:T(128)} %constant.134.clone.1), kind=kCustom, calls=%fused_computation.87 | custom fusion | bytes 4228
  152.1 0.7 reshape.374
  152.8 24.4 %reshape.360 = bf16[32,64,32,64]{3,2,1,0:T(8,128)(2,1)} reshape(bf16[2048,2048]{1,0:T(8,128)(2,1)} %all-gather.2.cloned.1.call-done) | data formatting | bytes 16777216 | tf_op jit(solution)/shard_map/reshape | solution.py:41
  177.2 17.5 %copy.133 = bf16[32,64,32,64]{3,1,2,0:T(8,128)(2,1)} copy(bf16[32,64,32,64]{3,2,1,0:T(8,128)(2,1)} %reshape.360) | data formatting | bytes 16777216 | tf_op jit(solution)/shard_map/reshape | solution.py:41
  194.7 338.0 %while.2 = (s32[]{:T(128)}, f32[4,256,64,64]{3,2,1,0:T(8,128)}, s32[4,256]{1,0:T(4,128)S(1)}, s32[4,256,4]{1,2,0:T(4,128)S(1)}, bf16[32,64,32,64]{3,1,2,0:T(8,12...) while((s32[]{:T(128)}, f32[4,256,64,64]{3,2,1,0:T(8,128)}, ...), condition=%wide.region_4.5_spmd, body=%wide.region_3.4_spmd.sunk | while | flops 536884736 | bytes 109128296 | solution.py:28
  195.1 20.4 %gather_fusion = bf16[1024,64,64]{2,1,0:T(8,128)(2,1)} fusion(bf16[32,64,32,64]{3,1,2,0:T(8,128)(2,1)} %get-tuple-element.207, s32[1024]{0:T(1024)S(1)} %reshape.481), kind=kCustom, calls=%fused_computation.clone.1 | custom fusion | bytes 16785408 | tf_op jit(solution)/shard_map/while/body/eval_jaxpr/gather | solution.py:15
  215.5 11.1 %gather_fusion.1 = bf16[256,64,256]{2,1,0:T(8,128)(2,1)} fusion(bf16[1,128,64,256]{3,2,1,0:T(8,128)(2,1)} %get-tuple-element.210, s32[256]{0:T(256)S(1)} %bitcast.115), kind=kCustom, calls=%fused_computation.1.clone.1 | custom fusion | bytes 16779264 | tf_op jit(solution)/shard_map/while/body/eval_jaxpr/gather | solution.py:83
  226.6 12.8 %copy.174 = bf16[256,64,256]{0,2,1:T(8,128)(2,1)} copy(bf16[256,64,256]{2,1,0:T(8,128)(2,1)} %gather_fusion.1) | data formatting | bytes 16777216 | tf_op jit(solution)/shard_map/while/body/eval_jaxpr/gather | solution.py:83
  239.5 24.0 %copy.175 = bf16[256,64,4,64]{3,1,2,0:T(8,128)(2,1)} copy(bf16[256,64,4,64]{0,3,2,1:T(8,128)(2,1)} %bitcast.114) | data formatting | bytes 16777216 | tf_op jit(solution)/shard_map/while/body/eval_jaxpr/reshape | solution.py:16
  263.5 15.8 %bitcast_dynamic-update-slice_fusion.2 = f32[4,256,64,64]{3,2,1,0:T(8,128)} fusion(f32[4,256,64,64]{3,2,1,0:T(8,128)} %get-tuple-element.195, s32[]{:T(128)} %get-tuple-element.194, bf16[256,4,64,64]{3,2,1,0:T(8,128)(2,1)} %bitcast.113, bf16[256,64,4,64]{3,1,2,0:T(8,128)(2,1)} %copy.175), kind=kOutput, calls=%fused_computation.8.clone.1 | convolution fusion | flops 536870912 | bytes 41943552 | tf_op jit(solution)/shard_map/while/body/eval_jaxpr/mxkc,mjkyc->mjyx/dot_general | solution.py:17
  279.6 20.4 %gather_fusion = bf16[1024,64,64]{2,1,0:T(8,128)(2,1)} fusion(bf16[32,64,32,64]{3,1,2,0:T(8,128)(2,1)} %get-tuple-element.207, s32[1024]{0:T(1024)S(1)} %reshape.481), kind=kCustom, calls=%fused_computation.clone.1 | custom fusion | bytes 16785408 | tf_op jit(solution)/shard_map/while/body/eval_jaxpr/gather | solution.py:15
  300.0 11.1 %gather_fusion.1 = bf16[256,64,256]{2,1,0:T(8,128)(2,1)} fusion(bf16[1,128,64,256]{3,2,1,0:T(8,128)(2,1)} %get-tuple-element.210, s32[256]{0:T(256)S(1)} %bitcast.115), kind=kCustom, calls=%fused_computation.1.clone.1 | custom fusion | bytes 16779264 | tf_op jit(solution)/shard_map/while/body/eval_jaxpr/gather | solution.py:83
  311.2 12.8 %copy.174 = bf16[256,64,256]{0,2,1:T(8,128)(2,1)} copy(bf16[256,64,256]{2,1,0:T(8,128)(2,1)} %gather_fusion.1) | data formatting | bytes 16777216 | tf_op jit(solution)/shard_map/while/body/eval_jaxpr/gather | solution.py:83
  324.0 24.0 %copy.175 = bf16[256,64,4,64]{3,1,2,0:T(8,128)(2,1)} copy(bf16[256,64,4,64]{0,3,2,1:T(8,128)(2,1)} %bitcast.114) | data formatting | bytes 16777216 | tf_op jit(solution)/shard_map/while/body/eval_jaxpr/reshape | solution.py:16
  348.0 15.8 %bitcast_dynamic-update-slice_fusion.2 = f32[4,256,64,64]{3,2,1,0:T(8,128)} fusion(f32[4,256,64,64]{3,2,1,0:T(8,128)} %get-tuple-element.195, s32[]{:T(128)} %get-tuple-element.194, bf16[256,4,64,64]{3,2,1,0:T(8,128)(2,1)} %bitcast.113, bf16[256,64,4,64]{3,1,2,0:T(8,128)(2,1)} %copy.175), kind=kOutput, calls=%fused_computation.8.clone.1 | convolution fusion | flops 536870912 | bytes 41943552 | tf_op jit(solution)/shard_map/while/body/eval_jaxpr/mxkc,mjkyc->mjyx/dot_general | solution.py:17
  364.1 20.4 %gather_fusion = bf16[1024,64,64]{2,1,0:T(8,128)(2,1)} fusion(bf16[32,64,32,64]{3,1,2,0:T(8,128)(2,1)} %get-tuple-element.207, s32[1024]{0:T(1024)S(1)} %reshape.481), kind=kCustom, calls=%fused_computation.clone.1 | custom fusion | bytes 16785408 | tf_op jit(solution)/shard_map/while/body/eval_jaxpr/gather | solution.py:15
  384.5 11.1 %gather_fusion.1 = bf16[256,64,256]{2,1,0:T(8,128)(2,1)} fusion(bf16[1,128,64,256]{3,2,1,0:T(8,128)(2,1)} %get-tuple-element.210, s32[256]{0:T(256)S(1)} %bitcast.115), kind=kCustom, calls=%fused_computation.1.clone.1 | custom fusion | bytes 16779264 | tf_op jit(solution)/shard_map/while/body/eval_jaxpr/gather | solution.py:83
  395.6 12.8 %copy.174 = bf16[256,64,256]{0,2,1:T(8,128)(2,1)} copy(bf16[256,64,256]{2,1,0:T(8,128)(2,1)} %gather_fusion.1) | data formatting | bytes 16777216 | tf_op jit(solution)/shard_map/while/body/eval_jaxpr/gather | solution.py:83
  408.5 24.0 %copy.175 = bf16[256,64,4,64]{3,1,2,0:T(8,128)(2,1)} copy(bf16[256,64,4,64]{0,3,2,1:T(8,128)(2,1)} %bitcast.114) | data formatting | bytes 16777216 | tf_op jit(solution)/shard_map/while/body/eval_jaxpr/reshape | solution.py:16
  432.5 15.8 %bitcast_dynamic-update-slice_fusion.2 = f32[4,256,64,64]{3,2,1,0:T(8,128)} fusion(f32[4,256,64,64]{3,2,1,0:T(8,128)} %get-tuple-element.195, s32[]{:T(128)} %get-tuple-element.194, bf16[256,4,64,64]{3,2,1,0:T(8,128)(2,1)} %bitcast.113, bf16[256,64,4,64]{3,1,2,0:T(8,128)(2,1)} %copy.175), kind=kOutput, calls=%fused_computation.8.clone.1 | convolution fusion | flops 536870912 | bytes 41943552 | tf_op jit(solution)/shard_map/while/body/eval_jaxpr/mxkc,mjkyc->mjyx/dot_general | solution.py:17
  448.6 20.4 %gather_fusion = bf16[1024,64,64]{2,1,0:T(8,128)(2,1)} fusion(bf16[32,64,32,64]{3,1,2,0:T(8,128)(2,1)} %get-tuple-element.207, s32[1024]{0:T(1024)S(1)} %reshape.481), kind=kCustom, calls=%fused_computation.clone.1 | custom fusion | bytes 16785408 | tf_op jit(solution)/shard_map/while/body/eval_jaxpr/gather | solution.py:15
  469.1 11.1 %gather_fusion.1 = bf16[256,64,256]{2,1,0:T(8,128)(2,1)} fusion(bf16[1,128,64,256]{3,2,1,0:T(8,128)(2,1)} %get-tuple-element.210, s32[256]{0:T(256)S(1)} %bitcast.115), kind=kCustom, calls=%fused_computation.1.clone.1 | custom fusion | bytes 16779264 | tf_op jit(solution)/shard_map/while/body/eval_jaxpr/gather | solution.py:83
  480.2 12.8 %copy.174 = bf16[256,64,256]{0,2,1:T(8,128)(2,1)} copy(bf16[256,64,256]{2,1,0:T(8,128)(2,1)} %gather_fusion.1) | data formatting | bytes 16777216 | tf_op jit(solution)/shard_map/while/body/eval_jaxpr/gather | solution.py:83
  493.0 24.0 %copy.175 = bf16[256,64,4,64]{3,1,2,0:T(8,128)(2,1)} copy(bf16[256,64,4,64]{0,3,2,1:T(8,128)(2,1)} %bitcast.114) | data formatting | bytes 16777216 | tf_op jit(solution)/shard_map/while/body/eval_jaxpr/reshape | solution.py:16
  517.0 15.8 %bitcast_dynamic-update-slice_fusion.2 = f32[4,256,64,64]{3,2,1,0:T(8,128)} fusion(f32[4,256,64,64]{3,2,1,0:T(8,128)} %get-tuple-element.195, s32[]{:T(128)} %get-tuple-element.194, bf16[256,4,64,64]{3,2,1,0:T(8,128)(2,1)} %bitcast.113, bf16[256,64,4,64]{3,1,2,0:T(8,128)(2,1)} %copy.175), kind=kOutput, calls=%fused_computation.8.clone.1 | convolution fusion | flops 536870912 | bytes 41943552 | tf_op jit(solution)/shard_map/while/body/eval_jaxpr/mxkc,mjkyc->mjyx/dot_general | solution.py:17
  532.8 17.8 %multiply_convert_fusion = bf16[32,32,64,64]{3,2,1,0:T(8,128)(2,1)} fusion(f32[32,32,64,64]{3,2,1,0:T(8,128)} %bitcast.120, f32[32,32]{1,0:T(8,128)S(1)} %bitcast.127), kind=kLoop, calls=%fused_computation.25 | loop fusion | flops 8388608 | bytes 25169920 | tf_op jit(solution)/shard_map/convert_element_type | solution.py:97
  550.6 26.7 %reshape.470 = bf16[32,2,65536]{2,1,0:T(2,128)(2,1)} reshape(bf16[32,32,64,64]{3,2,1,0:T(8,128)(2,1)} %multiply_convert_fusion) | data formatting | bytes 16777216
  577.3 7.8 all-to-all-start
  586.3 6.9 copy.134
  593.1 1.2 reduce-window.16
  595.3 13.0 %copy.157 = bf16[128,64,4,64,1]{3,1,2,4,0:T(8,128)(2,1)} copy(bf16[128,64,4,64,1]{0,3,2,1,4:T(8,128)(2,1)} %bitcast.121) | data formatting | bytes 8388608 | tf_op jit(solution)/shard_map/while/body/eval_jaxpr/reshape | solution.py:16
  608.4 34.8 %gather_fusion.2 = bf16[2048,64,64]{2,1,0:T(8,128)(2,1)} fusion(bf16[32,64,32,64]{3,1,2,0:T(8,128)(2,1)} %get-tuple-element.213, s32[2048]{0:T(1024)S(1)} %reshape.391), kind=kCustom, calls=%fused_computation.2 | custom fusion | bytes 33570816 | tf_op jit(solution)/shard_map/while/body/eval_jaxpr/gather | solution.py:15
  643.1 66.3 %all-to-all-done = bf16[32,2,65536]{2,1,0:T(2,128)(2,1)} async-done(((bf16[32,2,65536]{2,1,0:T(2,128)(2,1)}), bf16[32,2,65536]{2,1,0:T(2,128)(2,1)}, u32[]{:S(2)}, u32[]{:S(2)}) %all-to-all-start) | async-done | bytes 8388640 | tf_op jit(solution)/shard_map/all_to_all | solution.py:99
  709.5 26.0 %reshape.471 = bf16[32,32,64,64]{3,2,1,0:T(8,128)(2,1)} reshape(bf16[32,2,65536]{2,1,0:T(2,128)(2,1)} %all-to-all-done) | data formatting | bytes 16777216
  735.5 13.3 %gather_fusion.5 = bf16[512,64,64]{2,1,0:T(8,128)(2,1)} fusion(bf16[32,32,64,64]{3,2,1,0:T(8,128)(2,1)} %reshape.471, s32[512]{0:T(512)S(1)} %bitcast.119), kind=kCustom, calls=%fused_computation.5 | custom fusion | bytes 8392704 | tf_op jit(solution)/shard_map/gather | solution.py:106
  748.8 9.8 %copy.152 = bf16[512,64,64]{0,2,1:T(8,128)(2,1)} copy(bf16[512,64,64]{2,1,0:T(8,128)(2,1)} %gather_fusion.5) | data formatting | bytes 8388608 | tf_op jit(solution)/shard_map/gather | solution.py:106
  758.6 15.1 %copy.162 = f32[512,64,64]{1,2,0:T(8,128)} copy(bf16[512,64,64]{0,2,1:T(8,128)(2,1)} %copy.152) | data formatting | bytes 12582912 | tf_op jit(solution)/shard_map/convert_element_type | solution.py:107
  773.7 26.7 %bitcast_add_fusion = f32[128,4,64,64]{2,3,1,0:T(8,128)} fusion(f32[128,4,64,64]{2,3,1,0:T(8,128)} %bitcast.117, bf16[128,4,4,64,64]{4,3,2,1,0:T(8,128)(2,1)} %bitcast.116, bf16[128,64,4,64,1]{3,1,2,4,0:T(8,128)(2,1)} %copy.157), kind=kOutput, calls=%fused_computation.26 | convolution fusion | flops 1075838976 | bytes 37748736 | tf_op jit(solution)/shard_map/while/body/eval_jaxpr/mxkc,mjkyc->mjxy/dot_general | solution.py:17
  800.5 12.7 %copy.155 = f32[1,128,64,256]{3,2,1,0:T(8,128)} copy(f32[1,128,64,256]{2,3,1,0:T(8,128)} %bitcast.118) | data formatting | bytes 16777216 | tf_op jit(solution)/shard_map/reshape | solution.py:109
  (90 shorter events, 5.8 us)
Async XLA Ops:
  6.5 68.0 %copy-start = (s32[32,128,4]{1,2,0:T(4,128)S(1)}, s32[32,128,4]{1,2,0:T(4,128)}, u32[]{:S(2)}) copy-start(s32[32,128,4]{1,2,0:T(4,128)} %param.7) | copy-start | bytes 196612
  6.5 146.3 %all-gather.2.cloned.1.call-start = ((), (), s32[]{:S(2)}) async-start(), calls=%async_computation.1 | async-start | bytes 8454144 | tf_op jit(solution)/shard_map/all_gather | solution.py:40
  194.7 338.0 %copy-start.1 = (f32[32,33]{1,0:T(8,128)S(1)}, f32[32,33]{1,0:T(8,128)}, u32[]{:S(2)}) copy-start(f32[32,33]{1,0:T(8,128)} %reshape.374) | copy-start | bytes 12676
  577.3 132.2 %all-to-all-start = ((bf16[32,2,65536]{2,1,0:T(2,128)(2,1)}), bf16[32,2,65536]{2,1,0:T(2,128)(2,1)}, u32[]{:S(2)}, u32[]{:S(2)}) async-start(bf16[32,2,65536]{2,1,0:T(2,128)(2,1)} %reshape.470), calls=%async_computation | async-start | bytes 16777216 | tf_op jit(solution)/shard_map/all_to_all | solution.py:99
Sparse Core Ops, SparseCore 0:
  10.3 69.1 all-gather.1
where the time goes:
time: 827 us; the launch traced here: 820 us
  local copies, waits for them, and re-layouts  617 us (75%)
  matrix products  89.8 us (11%)
  waiting for transfers between devices  67.1 us (8%)
  other arithmetic  24 us (3%)
  between operations  13.6 us (2%)
    unnamed x17, local copies, waits for them, and re-layouts  182 us
    gather x5, local copies, waits for them, and re-layouts, dress_tiles(): chosen = fock_tiles[targets[:, :, None], :, col_list[:, None, :], :]  116 us
    reshape x5, local copies, waits for them, and re-layouts, dress_tiles(): split_rows = tile_rows.reshape(count, tile_size, kept_count, tile_size)  109 us
    gather x8, local copies, waits for them, and re-layouts, mirror_block(): tile_rows = amps[tile_index, row_index]  95.8 us
    dot_general x5, matrix products, dress_tiles(): jnp.einsum('mxkc,mjkyc->' + out_form, split_rows, chosen, preferred_eleme...  89.8 us
    all_to_all x1, waiting for transfers between devices, per_device(): lax.all_to_all(outgoing, 'virt', split_axis=0, concat_axis=0, tiled=True)  66.3 us
    reshape x2, local copies, waits for them, and re-layouts, per_device(): fock_tiles = full_fock.reshape(ntiles, tile_size, ntiles, tile_size)  41.9 us
    gather x2, local copies, waits for them, and re-layouts, per_device(): returned = received[source_tile, arrival_slot]  23.1 us
  transfers between devices with their start and end apart: 2, of which 1 were waited for; matrix products, arithmetic and copies ran while one was open for 25% of the time, Pallas kernels for 0%

commit v1 on v0

v1 whole, which is shorter than its diff:
```python
import functools

import jax
import jax.numpy as jnp
from jax import lax
from jax.experimental import pallas as pl
from jax.experimental.pallas import tpu as pltpu
from jax.sharding import PartitionSpec as P

MESH = pl.DeviceIdType.MESH
TILE = 64
KEPT = 4
ROWS = 128
NTILES = 32
NSIDE = 4
SPLITS = 4
SLOTS = 32
PER = SLOTS // SPLITS
PARTS = ((0, 5, "zyx"), (5, 5, "xzy"), (10, 6, "yxz"))
LANES = 16


def place(pos):
    return (pos["z"], pos["x"] * 8 + pos["y"] * 2 + pos["c"])


def moved(pos, axis, by):
    new = dict(pos)
    new[axis] = lax.rem(pos[axis] + by + 4, 4)
    return new


def exchange_kernel(
    rows_ref, cols_ref, at_ref, fock_ref, amps_ref, own_hbm, recv_hbm,
    ff, send, own, gsend, grecv, csend, crecv, tsend, trecv, lsem,
):
    zi = lax.axis_index("pairs")
    vi = lax.axis_index("virt")
    pos = {"x": vi // 8, "y": lax.rem(vi // 2, 4), "z": zi, "c": lax.rem(vi, 2)}

    def peer(off):
        px = lax.rem(pos["x"] + off // 8, 4)
        py = lax.rem(pos["y"] + lax.rem(off // 2, 4), 4)
        pc = lax.rem(pos["c"] + lax.rem(off, 2), 2)
        return px * 8 + py * 2 + pc

    def home(where, full, lo, width):
        z, x = [slice(None) if axis in full else where[axis] for axis in "zx"]
        high, low_y = slice(None), slice(None)
        if "y" not in full:
            high, low_y = where["y"] // 2, lax.rem(where["y"], 2)
        return ff.at[pl.ds(lo, width), z, x, high, low_y, where["c"]]

    barrier = pltpu.get_barrier_semaphore()

    def greet(off, carry):
        pl.semaphore_signal(barrier, inc=1, device_id=(zi, peer(off)), device_id_type=MESH)
        return carry

    lax.fori_loop(1, NTILES, greet, 0)
    for by in (1, 2, 3):
        pl.semaphore_signal(
            barrier, inc=1, device_id=place(moved(pos, "z", by)), device_id_type=MESH
        )
    mine = pltpu.make_async_copy(fock_ref, home(pos, "", 0, LANES), lsem)
    mine.start()
    mine.wait()
    pl.semaphore_wait(barrier, NTILES - 1 + 3)

    def block(part, where, full):
        lo, width, _ = PARTS[part]
        return home(where, full, lo, width)

    def push(part, number, where, full, axis, by):
        target = moved(pos, axis, by)
        ref = block(part, where, full)
        copy = pltpu.make_async_remote_copy(
            src_ref=ref, dst_ref=ref, send_sem=gsend.at[part, number],
            recv_sem=grecv.at[part, number], device_id=place(target), device_id_type=MESH,
        )
        copy.start()
        sent.append(copy)

    def arrived(part, number, where, full):
        ref = block(part, where, full)
        pltpu.make_async_remote_copy(
            src_ref=ref, dst_ref=ref, send_sem=gsend.at[part, number],
            recv_sem=grecv.at[part, number], device_id=place(moved(pos, "z", 1)),
            device_id_type=MESH,
        ).wait_recv()

    twin = {**pos, "c": 1 - pos["c"]}

    def across(part, number, where, full):
        ref = block(part, where, full)
        copy = pltpu.make_async_remote_copy(
            src_ref=ref, dst_ref=ref, send_sem=csend.at[part, number],
            recv_sem=crecv.at[part, number], device_id=place(twin), device_id_type=MESH,
        )
        copy.start()
        sent.append(copy)

    def came_across(part, number, where, full):
        ref = block(part, {**where, "c": twin["c"]}, full)
        pltpu.make_async_remote_copy(
            src_ref=ref, dst_ref=ref, send_sem=csend.at[part, number],
            recv_sem=crecv.at[part, number], device_id=place(twin), device_id_type=MESH,
        ).wait_recv()

    sent = []
    every = range(len(PARTS))
    for part in every:
        first = PARTS[part][2][0]
        for by in (1, 2, 3):
            push(part, by - 1, pos, "", first, by)
    for part in every:
        first, second, third = PARTS[part][2]
        for by in (1, 2, 3):
            arrived(part, by - 1, moved(pos, first, -by), "")
        for by in (1, 2, 3):
            push(part, 2 + by, pos, first, second, by)
        for by in (1, 2, 3):
            push(part, 5 + by, pos, first, third, by)
        across(part, 0, pos, first)
    for back in (1, 2, 3):
        for part in every:
            first, second, third = PARTS[part][2]
            where = moved(pos, second, -back)
            arrived(part, 2 + back, where, first)
            for by in (1, 2, 3):
                push(part, 5 + 3 * back + by, where, first, third, by)
            across(part, back, where, first)
    for back in range(4):
        for part in every:
            first, second, third = PARTS[part][2]
            where = moved(pos, second, -back)
            for by in (1, 2, 3):
                there = moved(where, third, -by)
                arrived(part, 5 + 3 * back + by, there, first)
                across(part, 4 * by + back, there, first)
    for back in range(4):
        for part in every:
            first, second, third = PARTS[part][2]
            where = moved(pos, second, -back)
            for by in range(4):
                came_across(part, 4 * by + back, moved(where, third, -by), first)
    for copy in sent:
        copy.wait_send()

    def swap_halves(s, carry):
        at = (s // 8, lax.rem(s // 2, 4), lax.rem(s, 2))
        for t in range(LANES):
            got = ff[(t,) + at].reshape(TILE, 128)
            turned = jnp.concatenate([got[:, TILE:], got[:, :TILE]], axis=1)
            ff[(LANES + t,) + at] = turned.reshape(2, 2, 16, 128)
        return carry

    lax.fori_loop(0, NTILES, swap_halves, 0)

    low = lax.broadcasted_iota(jnp.int32, (TILE, 128), 1) < TILE

    def tile_row(tile, cols):
        got = [ff[(col,) + tile].reshape(TILE, 128) for col in cols]
        return jnp.concatenate(
            [jnp.where(low, got[0], got[1]), jnp.where(low, got[2], got[3])], axis=1
        )

    def dressed(tile, slot):
        row = rows_ref[tile * SLOTS + slot]
        cols = [cols_ref[row, k] for k in range(KEPT)]
        at = (tile // 8, lax.rem(tile // 2, 4), lax.rem(tile, 2))
        return lax.dot_general(
            tile_row(at, cols), amps_ref[row], (((1,), (1,)), ((), ())),
            preferred_element_type=jnp.float32,
        )

    def tile_copy(step, tile, split):
        return pltpu.make_async_remote_copy(
            src_ref=send.at[step], dst_ref=recv_hbm.at[vi, split], send_sem=tsend.at[step],
            recv_sem=trecv.at[step], device_id=(zi, tile), device_id_type=MESH,
        )

    def offset_of(step):
        return lax.rem(lax.rem(step, 32) * 13 + 13, 32)

    def mirror(step, carry):
        split = step // 32
        off = offset_of(step)
        tile = peer(off)
        for s in range(0, PER, 2):
            pair = [dressed(tile, split * PER + s + i).astype(jnp.bfloat16) for i in (0, 1)]
            send[step, s // 2] = jnp.concatenate(pair, axis=1)

        @pl.when(off != 0)
        def _():
            tile_copy(step, tile, split).start()

        @pl.when(off == 0)
        def _():
            pltpu.make_async_copy(
                send.at[step], recv_hbm.at[vi, split], tsend.at[step]
            ).start()

        return carry

    lax.fori_loop(0, NTILES * SPLITS, mirror, 0)

    def own_row(row, carry):
        cols = [cols_ref[row, k] for k in range(KEPT)]
        tiles = [tuple(at_ref[i, row, k] for i in range(3)) for k in range(KEPT)]
        weights = jnp.concatenate([tile_row(tile, cols) for tile in tiles], axis=0)
        own[row] = lax.dot_general(
            amps_ref[row], weights, (((1,), (1,)), ((), ())), preferred_element_type=jnp.float32
        )
        return carry

    lax.fori_loop(0, ROWS, own_row, 0)
    out_copy = pltpu.make_async_copy(own, own_hbm, lsem)
    out_copy.start()

    def finish(step, carry):
        split = step // 32
        off = offset_of(step)

        @pl.when(off != 0)
        def _():
            copy = tile_copy(step, peer(off), split)
            copy.wait_send()
            copy.wait_recv()

        @pl.when(off == 0)
        def _():
            pltpu.make_async_copy(
                send.at[step], recv_hbm.at[vi, split], tsend.at[step]
            ).wait()

        return carry

    lax.fori_loop(0, NTILES * SPLITS, finish, 0)
    out_copy.wait()


def combine_kernel(slot_ref, turn_ref, own_ref, recv_ref, out_ref):
    low = lax.broadcasted_iota(jnp.int32, (TILE, 128), 1) < TILE
    count = own_ref.shape[0]
    base = pl.program_id(0) * count
    for r in range(count):
        for h in range(2):
            halves = []
            for i in range(2):
                at = (base + r) * KEPT + 2 * h + i
                got = recv_ref[slot_ref[at]].astype(jnp.float32)
                halves.append(pltpu.roll(got, turn_ref[at], axis=1))
            out_ref[r, :, h * 128:(h + 1) * 128] = own_ref[r, :, h * 128:(h + 1) * 128] + jnp.where(
                low, halves[0], halves[1]
            )


def tables(cols, me):
    count = cols.shape[1]
    order = jnp.arange(count)
    named = jnp.any(cols == me, axis=2).astype(jnp.float32)
    upto = jnp.dot(named, (order[:, None] <= order[None, :]).astype(jnp.float32))
    slots = jnp.arange(SLOTS, dtype=jnp.float32)
    rank = jnp.sum((upto[:, None, :] <= slots[None, :, None]).astype(jnp.int32), axis=2)
    rows = count - 1 - jnp.minimum(rank, count - 1)
    my_cols = lax.dynamic_index_in_dim(cols, me, 0, keepdims=False)
    hot = (my_cols[:, :, None] == jnp.arange(NTILES, dtype=jnp.int32)).astype(jnp.float32)
    before = jnp.dot((order[:, None] > order[None, :]).astype(jnp.float32), jnp.sum(hot, axis=1))
    slot = jnp.sum(hot * before[:, None, :], axis=2).astype(jnp.int32)
    at = my_cols * (SLOTS // 2) + slot // 2
    turn = ((slot + jnp.arange(KEPT, dtype=jnp.int32)) % 2) * TILE
    version = (my_cols + jnp.arange(KEPT, dtype=jnp.int32)) % 2
    places = version * LANES + my_cols // 2
    parts = jnp.stack([my_cols // 8, my_cols // 2 % 4, my_cols % 2])
    return rows.reshape(-1), places, parts, at.reshape(-1), turn.reshape(-1)


def per_device(amps, fock, cols):
    me = lax.axis_index("virt")
    rows, places, parts, at, turn = tables(cols, me)
    vmem = pl.BlockSpec(memory_space=pltpu.VMEM)
    smem = pl.BlockSpec(memory_space=pltpu.SMEM)
    anywhere = pl.BlockSpec(memory_space=pl.ANY)
    own, received = pl.pallas_call(
        exchange_kernel,
        out_shape=(
            jax.ShapeDtypeStruct((ROWS, TILE, KEPT * TILE), jnp.float32),
            jax.ShapeDtypeStruct((NTILES, SPLITS, PER // 2, TILE, 2 * TILE), jnp.bfloat16),
        ),
        in_specs=[smem, smem, smem, anywhere, vmem],
        out_specs=(anywhere, anywhere),
        scratch_shapes=[
            pltpu.VMEM((2 * LANES, 4, 4, 2, 2, 2, 16, 128), jnp.bfloat16),
            pltpu.VMEM((NTILES * SPLITS, PER // 2, TILE, 2 * TILE), jnp.bfloat16),
            pltpu.VMEM((ROWS, TILE, KEPT * TILE), jnp.float32),
            pltpu.SemaphoreType.DMA((3, 18)),
            pltpu.SemaphoreType.DMA((3, 18)),
            pltpu.SemaphoreType.DMA((3, 16)),
            pltpu.SemaphoreType.DMA((3, 16)),
            pltpu.SemaphoreType.DMA((NTILES * SPLITS,)),
            pltpu.SemaphoreType.DMA((NTILES * SPLITS,)),
            pltpu.SemaphoreType.DMA,
        ],
        compiler_params=pltpu.CompilerParams(
            collective_id=0, has_side_effects=True, vmem_limit_bytes=50 * 2**20
        ),
    )(
        rows, places, parts, fock.reshape(16, LANES, 128).transpose(1, 0, 2),
        amps.reshape(ROWS, TILE, KEPT * TILE),
    )
    step = 8
    blocked = pl.BlockSpec((step, TILE, KEPT * TILE), lambda i: (i, 0, 0))
    out = pl.pallas_call(
        combine_kernel,
        grid=(ROWS // step,),
        out_shape=jax.ShapeDtypeStruct((ROWS, TILE, KEPT * TILE), jnp.float32),
        in_specs=[smem, smem, blocked, vmem],
        out_specs=blocked,
        compiler_params=pltpu.CompilerParams(vmem_limit_bytes=32 * 2**20),
    )(at, turn, own, received.reshape(NTILES * SLOTS // 2, TILE, 2 * TILE))
    return out[None]


def solution(mesh):
    in_specs = (P("virt", "pairs", None, None), P(("pairs", "virt"), None), P(None, "pairs", None))
    out_specs = P("virt", "pairs", None, None)
    return jax.shard_map(
        per_device, mesh=mesh, in_specs=in_specs, out_specs=out_specs, check_vma=False
    )
```

time: 827 us -> 175 us (0.21)
  the two profiles are of different devices: /device:TPU:72 before, /device:TPU:77 now
where the time goes in v1:
time: 175 us; the launch traced here: 174 us
  Pallas kernels  164 us (94%)
  local copies, waits for them, and re-layouts  7.7 us (4%)
  other arithmetic  2.44 us (1%)
    pallas_call x1, Pallas kernels, per_device(): pl.pallas_call(exchange_kernel, out_shape=(jax.ShapeDtypeStruct((ROWS, TI...  155 us
    pallas_call x1, Pallas kernels, per_device(): pl.pallas_call(combine_kernel, grid=(ROWS // step,), out_shape=jax.ShapeD...  8.89 us
    unnamed x6, local copies, waits for them, and re-layouts  6.76 us

profile of v1, /device:TPU:77, one launch (start us, length us, event | category | flops | bytes accessed | tf_op | source)
XLA Modules:
  0.0 174.5 jit_solution(17775149553735389861)
XLA Ops:
  0.0 0.0 copy-start
  0.0 0.9 compare_reduce_fusion
  0.9 0.7 add_select_fusion.5
  1.7 0.1 fusion.5
  1.8 0.6 convert_reduce_fusion
  2.4 0.1 sub.27.rows_ref
  2.5 0.1 copy.15
  2.6 0.1 copy.16
  2.7 0.1 fusion.4
  2.9 0.1 copy.17
  3.0 0.1 convert_element_type.19
  3.1 0.1 fusion.2.cols_ref
  3.2 0.1 copy.14
  3.3 0.1 mul.26
  3.4 0.0 copy-done
  3.5 0.1 add.60
  3.6 0.1 copy.19.at_ref
  3.7 155.1 %shard_map.37 = (f32[128,64,256]{2,1,0:T(8,128)}, bf16[32,4,4,64,128]{4,3,2,1,0:T(8,128)(2,1)}) custom-call(s32[1024]{0:T(1024)S(1)} %sub.27.rows_ref, s32[128,4]{1,0:T(8,128)S(1)} %fusion.2.cols_ref, s32[3,128,4]{2,1,0:T(8,128)S(1)} %copy.19.at_ref, bf16[16,16,128]{2,1,0:T(8,128)(2,1)S(1)} %bitcast_bitcast_fusion.fock_ref, bf16[128,64,256]{2,1,0:T(8,128)(2,1)} %bitcast.15), custom_call_target="tpu_custom_call" | custom-call | tf_op jit(solution)/shard_map/pallas_call | solution.py:285
  158.8 0.0 copy-start.1
  158.8 3.4 %copy-done.1 = f32[128,64,256]{2,1,0:T(8,128)S(1)} copy-done((f32[128,64,256]{2,1,0:T(8,128)S(1)}, f32[128,64,256]{2,1,0:T(8,128)}, u32[]{:S(2)}) %copy-start.1) | copy-done | bytes 8388632
  162.2 0.0 copy-start.2
  162.2 3.4 %copy-done.2 = bf16[32,4,4,64,128]{4,3,2,1,0:T(8,128)(2,1)S(1)} copy-done((bf16[32,4,4,64,128]{4,3,2,1,0:T(8,128)(2,1)S(1)}, bf16[32,4,4,64,128]{4,3,2,1,0:T(8,128)(2,1)}, u32[]{:S(2)}) %copy-start.2) | copy-done | bytes 8388632
  165.6 8.9 %shard_map.38 = f32[128,64,256]{2,1,0:T(8,128)} custom-call(s32[512]{0:T(512)S(1)} %get-tuple-element.15.slot_ref, s32[512]{0:T(512)S(1)} %get-tuple-element.14.turn_ref, f32[128,64,256]{2,1,0:T(8,128)S(1)} %copy-done.1, bf16[512,64,128]{2,1,0:T(8,128)(2,1)S(1)} %bitcast.14), custom_call_target="tpu_custom_call" | custom-call | tf_op jit(solution)/shard_map/pallas_call | solution.py:314
  (9 shorter events, 0.1 us)
Async XLA Ops:
  0.0 3.4 %copy-start = (bf16[16,2048]{1,0:T(8,128)(2,1)S(1)}, bf16[16,2048]{1,0:T(8,128)(2,1)}, u32[]{:S(2)}) copy-start(bf16[16,2048]{1,0:T(8,128)(2,1)} %param.4) | copy-start | bytes 196612
  158.8 3.4 %copy-start.1 = (f32[128,64,256]{2,1,0:T(8,128)S(1)}, f32[128,64,256]{2,1,0:T(8,128)}, u32[]{:S(2)}) copy-start(f32[128,64,256]{2,1,0:T(8,128)} %get-tuple-element.7.own_ref) | copy-start | bytes 25165828
  162.2 3.4 %copy-start.2 = (bf16[32,4,4,64,128]{4,3,2,1,0:T(8,128)(2,1)S(1)}, bf16[32,4,4,64,128]{4,3,2,1,0:T(8,128)(2,1)}, u32[]{:S(2)}) copy-start(bf16[32,4,4,64,128]{4,3,2,1,0:T(8,128)(2,1)} %get-tuple-element.8) | copy-start | bytes 25165828

commit v2 on v0

v2 whole, which is shorter than its diff:
```python
import functools

import jax
import jax.numpy as jnp
from jax import lax
from jax.experimental import pallas as pl
from jax.experimental.pallas import tpu as pltpu
from jax.sharding import PartitionSpec as P

MESH = pl.DeviceIdType.MESH
TILE = 64
KEPT = 4
ROWS = 128
NTILES = 32
NSIDE = 4
SPLITS = 4
SLOTS = 32
PER = SLOTS // SPLITS
LANES = 16
CHUNK = 16
HALF = 1024


def place(pos):
    return (pos["z"], pos["x"] * 8 + pos["y"] * 2 + pos["c"])


def moved(pos, axis, by):
    new = dict(pos)
    new[axis] = lax.rem(pos[axis] + by + 4, 4)
    return new


def write_tables(me, cols_ref, vtab, vown, back_ref):
    f32, bf16, i32 = jnp.float32, jnp.bfloat16, jnp.int32
    mine = cols_ref[me]
    kept = lax.broadcasted_iota(i32, (KEPT, ROWS), 0)
    lane = lax.broadcasted_iota(i32, (KEPT, ROWS), 1)
    mine = jnp.minimum(jnp.maximum(mine, 0), NTILES - 1)
    spot = ((mine + kept) & 1) * LANES + (mine >> 1)
    vown[...] = jnp.concatenate([spot, mine], axis=0)
    first = lax.broadcasted_iota(i32, (ROWS, ROWS), 0)
    second = lax.broadcasted_iota(i32, (ROWS, ROWS), 1)
    upper = (first <= second).astype(f32).astype(bf16)
    flip = (first + second == ROWS - 1).astype(f32).astype(bf16)
    about = jnp.concatenate([spot, lane], axis=0).astype(f32).astype(bf16)
    about = jnp.dot(about, flip, preferred_element_type=f32).astype(bf16)
    named = jnp.sum((cols_ref[...] == me).astype(f32), axis=1)
    upto = jnp.dot(named.astype(bf16), upper, preferred_element_type=f32)
    rank = jnp.where(named > 0, upto, 0.0)
    slots = lax.broadcasted_iota(i32, (SLOTS, ROWS), 0).astype(f32) + 1.0
    entry = lax.broadcasted_iota(i32, (8, 8 * SLOTS), 0)
    largest = jnp.where(entry < KEPT, 2 * LANES - 1, ROWS - 1)
    for peer in range(0, NTILES, 8):
        hot = [
            (jnp.broadcast_to(rank[p:p + 1], (SLOTS, ROWS)) == slots).astype(f32).astype(bf16)
            for p in range(peer, peer + 8)
        ]
        got = lax.dot_general(
            about, jnp.concatenate(hot, axis=0), (((1,), (1,)), ((), ())),
            preferred_element_type=f32,
        )
        got = jnp.minimum(jnp.maximum(got.astype(i32), 0), largest)
        vtab[:, peer * SLOTS:(peer + 8) * SLOTS] = got
    number = lax.broadcasted_iota(i32, (NTILES, ROWS), 0)
    at = [jnp.broadcast_to(mine[k:k + 1], (NTILES, ROWS)) == number for k in range(KEPT)]
    count = sum(hit.astype(f32) for hit in at)
    before = jnp.dot(count.astype(bf16), upper, preferred_element_type=f32) - count
    slot = [jnp.sum(jnp.where(hit, before, 0.0), axis=0, keepdims=True) for hit in at]
    slot = jnp.minimum(jnp.maximum(jnp.concatenate(slot, axis=0).astype(i32), 0), SLOTS - 1)
    back_ref[...] = jnp.concatenate(
        [mine * (SLOTS // 2) + (slot >> 1), ((slot + kept) & 1) * TILE], axis=0
    )


def exchange_kernel(
    cols_ref, fock_ref, amps_hbm, own_hbm, recv_hbm, back_ref,
    land, fa, amps, send, own, vtab, vown, stab, sown,
    gsend, grecv, csend, crecv, tsend, trecv, lsem,
):
    zi = lax.axis_index("pairs")
    vi = lax.axis_index("virt")
    pos = {"x": vi // 8, "y": lax.rem(vi // 2, 4), "z": zi, "c": lax.rem(vi, 2)}
    twin = {**pos, "c": 1 - pos["c"]}

    load_amps = pltpu.make_async_copy(amps_hbm, amps, lsem.at[0])
    load_amps.start()

    barrier = pltpu.get_barrier_semaphore()

    def greet(off, carry):
        pl.semaphore_signal(
            barrier, inc=1, device_id=(zi, lax.rem(vi + off, NTILES)), device_id_type=MESH
        )
        return carry

    lax.fori_loop(1, NTILES, greet, 0)
    for by in (1, 2, 3):
        pl.semaphore_signal(
            barrier, inc=1, device_id=place(moved(pos, "z", by)), device_id_type=MESH
        )
    land[pos["z"], pos["x"], pos["y"], pos["c"]] = fock_ref[...]
    pl.semaphore_wait(barrier, NTILES - 1 + 3)

    sent = []

    def rows_at(where, full, half):
        at = [slice(None) if axis in full else where[axis] for axis in "zxy"]
        cols = slice(None) if half is None else pl.ds(half * HALF, HALF)
        return land.at[at[0], at[1], at[2], where["c"], :, cols]

    def copy_to(target, number, src, dst, out=gsend, into=grecv):
        return pltpu.make_async_remote_copy(
            src_ref=src, dst_ref=dst, send_sem=out.at[number], recv_sem=into.at[number],
            device_id=place(target), device_id_type=MESH,
        )

    def push(axis, by, number, where, full="", half=None, own_rows=False):
        dst = rows_at(where, full, half)
        src = dst
        if own_rows:
            src = fock_ref if half is None else fock_ref.at[:, pl.ds(half * HALF, HALF)]
        copy = copy_to(moved(pos, axis, by), number, src, dst)
        copy.start()
        sent.append(copy)

    def arrived(number, where, full="", half=None):
        ref = rows_at(where, full, half)
        copy_to(twin, number, ref, ref).wait_recv()

    def across(number, where, full="", half=None):
        ref = rows_at(where, full, half)
        copy = copy_to(twin, number, ref, ref, csend, crecv)
        copy.start()
        sent.append(copy)

    def came_across(number, where, full="", half=None):
        ref = rows_at({**where, "c": twin["c"]}, full, half)
        copy_to(twin, number, ref, ref, csend, crecv).wait_recv()

    def far(g):
        return moved(pos, "x", -g)

    def far_first(g):
        arrived(g - 1, far(g))
        for by in (1, 2, 3):
            push("y", by, 15 + 6 * (g - 1) + by - 1, far(g))

    def far_second(g):
        for by in (1, 2, 3):
            arrived(15 + 6 * (g - 1) + by - 1, moved(far(g), "y", -by))
        for by in (1, 2, 3):
            push("z", by, 18 + 6 * (g - 1) + by - 1, far(g), "y")
        across(8 + 4 * (g - 1), far(g), "y")

    def far_third(g):
        for by in (1, 2, 3):
            there = moved(far(g), "z", -by)
            arrived(18 + 6 * (g - 1) + by - 1, there, "y")
            across(8 + 4 * (g - 1) + by, there, "y")

    def far_last(g):
        for by in range(4):
            came_across(8 + 4 * (g - 1) + by, moved(far(g), "z", -by), "y")

    for by in (1, 2, 3):
        push("z", by, 3 + by - 1, pos, half=0, own_rows=True)
        push("y", by, 6 + by - 1, pos, half=1, own_rows=True)
    for by in (1, 2, 3):
        push("x", by, by - 1, pos, own_rows=True)
    write_tables(vi, cols_ref, vtab, vown, back_ref)
    job_table = pltpu.make_async_copy(vtab, stab, lsem.at[1])
    own_table = pltpu.make_async_copy(vown, sown, lsem.at[2])
    job_table.start()
    own_table.start()
    for half, axis, other in ((0, "z", "y"), (1, "y", "z")):
        for by in (1, 2, 3):
            arrived(3 + 3 * half + by - 1, moved(pos, axis, -by), half=half)
        for by in (1, 2, 3):
            push(other, by, 9 + 3 * half + by - 1, pos, axis, half)
        across(4 * half, pos, axis, half)
    for g in (1, 2, 3):
        far_first(g)
    for by in (1, 2, 3):
        for half, axis, other in ((0, "z", "y"), (1, "y", "z")):
            there = moved(pos, other, -by)
            arrived(9 + 3 * half + by - 1, there, axis, half)
            across(4 * half + by, there, axis, half)
    far_second(1)
    for by in range(4):
        for half, axis, other in ((0, "z", "y"), (1, "y", "z")):
            came_across(4 * half + by, moved(pos, other, -by), axis, half)
    job_table.wait()
    own_table.wait()
    load_amps.wait()

    def spread(zs, xs, high):
        tile = zs * 8 + xs * 2 + high
        for part in range(4):
            for t in range(LANES):
                got = land[zs, xs, high * 2 + part // 2, part % 2, :, t * 128:(t + 1) * 128]
                fa[t, tile, part * 16:(part + 1) * 16] = got
                fa[LANES + t, tile, part * 16:(part + 1) * 16] = jnp.concatenate(
                    [got[:, TILE:], got[:, :TILE]], axis=1
                )

    low = lax.broadcasted_iota(jnp.int32, (TILE, 128), 1) < TILE

    def tile_row(tile, cols):
        got = [fa[col, tile] for col in cols]
        return jnp.concatenate(
            [jnp.where(low, got[0], got[1]), jnp.where(low, got[2], got[3])], axis=1
        )

    def dressed(tile, slot):
        at = tile * SLOTS + slot
        cols = [stab[k, at] for k in range(KEPT)]
        return lax.dot_general(
            tile_row(tile, cols), amps[stab[KEPT, at]], (((1,), (1,)), ((), ())),
            preferred_element_type=jnp.float32,
        )

    def tile_copy(tile, split):
        return pltpu.make_async_remote_copy(
            src_ref=send.at[tile, split], dst_ref=recv_hbm.at[vi, split],
            send_sem=tsend.at[tile * SPLITS + split], recv_sem=trecv.at[vi * SPLITS + split],
            device_id=(zi, tile), device_id_type=MESH,
        )

    def self_copy(split):
        return pltpu.make_async_copy(
            send.at[vi, split], recv_hbm.at[vi, split], tsend.at[vi * SPLITS + split]
        )

    def group(g):
        xs = lax.rem(pos["x"] + 4 - g, 4)

        def mirror(step, carry):
            split = step // 8
            at = lax.rem(step, 8)
            zs, high = lax.rem(pos["x"] + 1 + at // 2, 4), lax.rem(at, 2)
            tile = zs * 8 + xs * 2 + high

            @pl.when(split == 0)
            def _():
                spread(zs, xs, high)

            for s in range(0, PER, 2):
                pair = [dressed(tile, split * PER + s + i).astype(jnp.bfloat16) for i in (0, 1)]
                send[tile, split, s // 2] = jnp.concatenate(pair, axis=1)

            @pl.when(tile != vi)
            def _():
                tile_copy(tile, split).start()

            @pl.when(tile == vi)
            def _():
                self_copy(split).start()

            return carry

        lax.fori_loop(0, 8 * SPLITS, mirror, 0)

    group(0)
    far_third(1)
    far_second(2)
    far_last(1)
    group(1)
    far_third(2)
    far_second(3)
    far_last(2)
    group(2)
    far_third(3)
    far_last(3)
    group(3)

    def own_row(row, carry):
        cols = [sown[k, row] for k in range(KEPT)]
        weights = jnp.concatenate(
            [tile_row(sown[KEPT + k, row], cols) for k in range(KEPT)], axis=0
        )
        own[row] = lax.dot_general(
            amps[row], weights, (((1,), (1,)), ((), ())), preferred_element_type=jnp.float32
        )
        return carry

    lax.fori_loop(0, ROWS, own_row, 0)
    out_copy = pltpu.make_async_copy(own, own_hbm, lsem.at[0])
    out_copy.start()
    for copy in sent:
        copy.wait_send()

    def finish(step, carry):
        peer, split = step // SPLITS, lax.rem(step, SPLITS)

        @pl.when(peer != vi)
        def _():
            tile_copy(peer, split).wait_send()
            pltpu.make_async_remote_copy(
                src_ref=send.at[peer, split], dst_ref=recv_hbm.at[peer, split],
                send_sem=tsend.at[step], recv_sem=trecv.at[step],
                device_id=(zi, peer), device_id_type=MESH,
            ).wait_recv()

        @pl.when(peer == vi)
        def _():
            self_copy(split).wait()

        return carry

    lax.fori_loop(0, NTILES * SPLITS, finish, 0)
    out_copy.wait()


def combine_kernel(back_ref, own_hbm, recv_hbm, out_hbm, own, recv, in_sem, out_sem, recv_sem):
    load_recv = pltpu.make_async_copy(recv_hbm, recv, recv_sem)
    load_recv.start()

    def chunk(number):
        return pl.ds(pl.multiple_of(number * CHUNK, CHUNK), CHUNK)

    def load(number):
        return pltpu.make_async_copy(
            own_hbm.at[chunk(number)], own.at[chunk(number)], in_sem.at[number]
        )

    def store(number):
        return pltpu.make_async_copy(
            own.at[chunk(number)], out_hbm.at[chunk(number)], out_sem.at[number]
        )

    for number in range(ROWS // CHUNK):
        load(number).start()
    load_recv.wait()
    low = lax.broadcasted_iota(jnp.int32, (TILE, 128), 1) < TILE

    def part(number, carry):
        load(number).wait()

        def some_rows(some, carry):
            for r in range(4):
                row = number * CHUNK + some * 4 + r
                for h in range(2):
                    lanes = pl.ds(h * 128, 128)
                    left, right = [recv[back_ref[2 * h + i, row]] for i in range(2)]
                    turns = [back_ref[KEPT + 2 * h + i, row] for i in range(2)]
                    kept = jnp.where(low, left, right)
                    other = jnp.where(low, right, left)
                    other = jnp.concatenate([other[:, TILE:], other[:, :TILE]], axis=1)
                    stay = jnp.where(low, turns[0], turns[1]) == 0
                    own[row, :, lanes] += jnp.where(
                        stay, kept.astype(jnp.float32), other.astype(jnp.float32)
                    )
            return carry

        lax.fori_loop(0, CHUNK // 4, some_rows, 0)
        store(number).start()
        return carry

    lax.fori_loop(0, ROWS // CHUNK, part, 0)
    for number in range(ROWS // CHUNK):
        store(number).wait()


def per_device(amps, fock, cols):
    vmem = pl.BlockSpec(memory_space=pltpu.VMEM)
    smem = pl.BlockSpec(memory_space=pltpu.SMEM)
    anywhere = pl.BlockSpec(memory_space=pl.ANY)
    own, received, back = pl.pallas_call(
        exchange_kernel,
        out_shape=(
            jax.ShapeDtypeStruct((ROWS, TILE, KEPT * TILE), jnp.float32),
            jax.ShapeDtypeStruct((NTILES, SPLITS, PER // 2, TILE, 2 * TILE), jnp.bfloat16),
            jax.ShapeDtypeStruct((2 * KEPT, ROWS), jnp.int32),
        ),
        in_specs=[vmem, vmem, anywhere],
        out_specs=(anywhere, anywhere, vmem),
        scratch_shapes=[
            pltpu.VMEM((4, 4, 4, 2, 16, 2048), jnp.bfloat16),
            pltpu.VMEM((2 * LANES, NTILES, TILE, 128), jnp.bfloat16),
            pltpu.VMEM((ROWS, TILE, KEPT * TILE), jnp.bfloat16),
            pltpu.VMEM((NTILES, SPLITS, PER // 2, TILE, 2 * TILE), jnp.bfloat16),
            pltpu.VMEM((ROWS, TILE, KEPT * TILE), jnp.float32),
            pltpu.VMEM((8, NTILES * SLOTS), jnp.int32),
            pltpu.VMEM((8, ROWS), jnp.int32),
            pltpu.SMEM((8, NTILES * SLOTS), jnp.int32),
            pltpu.SMEM((8, ROWS), jnp.int32),
            pltpu.SemaphoreType.DMA((33,)),
            pltpu.SemaphoreType.DMA((33,)),
            pltpu.SemaphoreType.DMA((20,)),
            pltpu.SemaphoreType.DMA((20,)),
            pltpu.SemaphoreType.DMA((NTILES * SPLITS,)),
            pltpu.SemaphoreType.DMA((NTILES * SPLITS,)),
            pltpu.SemaphoreType.DMA((3,)),
        ],
        compiler_params=pltpu.CompilerParams(
            collective_id=0, has_side_effects=True, vmem_limit_bytes=58 * 2**20
        ),
    )(cols.transpose(0, 2, 1), fock, amps.reshape(ROWS, TILE, KEPT * TILE))
    out = pl.pallas_call(
        combine_kernel,
        out_shape=jax.ShapeDtypeStruct((ROWS, TILE, KEPT * TILE), jnp.float32),
        in_specs=[smem, anywhere, anywhere],
        out_specs=anywhere,
        scratch_shapes=[
            pltpu.VMEM((ROWS, TILE, KEPT * TILE), jnp.float32),
            pltpu.VMEM((NTILES * SLOTS // 2, TILE, 2 * TILE), jnp.bfloat16),
            pltpu.SemaphoreType.DMA((ROWS // CHUNK,)),
            pltpu.SemaphoreType.DMA((ROWS // CHUNK,)),
            pltpu.SemaphoreType.DMA,
        ],
        compiler_params=pltpu.CompilerParams(vmem_limit_bytes=58 * 2**20),
    )(back, own, received.reshape(NTILES * SLOTS // 2, TILE, 2 * TILE))
    return out[None]


def solution(mesh):
    in_specs = (P("virt", "pairs", None, None), P(("pairs", "virt"), None), P(None, "pairs", None))
    out_specs = P("virt", "pairs", None, None)
    return jax.shard_map(
        per_device, mesh=mesh, in_specs=in_specs, out_specs=out_specs, check_vma=False
    )
```

time: 827 us -> 151 us (0.18)
  the two profiles are of different devices: /device:TPU:72 before, /device:TPU:15 now
where the time goes in v2:
time: 151 us
  Pallas kernels  151 us (100%)
    pallas_call x1, Pallas kernels, per_device(): pl.pallas_call(exchange_kernel, out_shape=(jax.ShapeDtypeStruct((ROWS, TI...  140 us
    pallas_call x1, Pallas kernels, per_device(): pl.pallas_call(combine_kernel, out_shape=jax.ShapeDtypeStruct((ROWS, TILE...  11 us

profile of v2, /device:TPU:15, one launch (start us, length us, event | category | flops | bytes accessed | tf_op | source)
XLA Modules:
  0.0 150.9 jit_solution(18129267970146571857)
XLA Ops:
  0.0 139.9 %shard_map.37 = (f32[128,64,256]{2,1,0:T(8,128)}, bf16[32,4,4,64,128]{4,3,2,1,0:T(8,128)(2,1)}, s32[8,128]{1,0:T(8,128)}) custom-call(s32[32,4,128]{2,1,0:T(4,128)} %bitcast.6, bf16[16,2048]{1,0:T(8,128)(2,1)} %fock_ref.1, bf16[128,64,256]{2,1,0:T(8,128)(2,1)} %bitcast.5), custom_call_target="tpu_custom_call" | custom-call | tf_op jit(solution)/shard_map/pallas_call | solution.py:369
  139.9 11.0 %shard_map.38 = f32[128,64,256]{2,1,0:T(8,128)} custom-call(s32[8,128]{1,0:T(8,128)} %get-tuple-element.8.back_ref, f32[128,64,256]{2,1,0:T(8,128)} %get-tuple-element.9.own_hbm, bf16[512,64,128]{2,1,0:T(8,128)(2,1)} %bitcast.4), custom_call_target="tpu_custom_call" | custom-call | tf_op jit(solution)/shard_map/pallas_call | solution.py:400

commit v3 on v2

--- a/solution.py
+++ b/solution.py
@@ -74,8 +74,8 @@
 
 
 def exchange_kernel(
-    cols_ref, fock_ref, amps_hbm, own_hbm, recv_hbm, back_ref,
-    land, fa, amps, send, own, vtab, vown, stab, sown,
+    cols_ref, fock_ref, amps_hbm, own, recv, back_ref,
+    land, fa, amps, send, vtab, vown, stab, sown,
     gsend, grecv, csend, crecv, tsend, trecv, lsem,
 ):
     zi = lax.axis_index("pairs")
@@ -222,14 +222,14 @@
 
     def tile_copy(tile, split):
         return pltpu.make_async_remote_copy(
-            src_ref=send.at[tile, split], dst_ref=recv_hbm.at[vi, split],
+            src_ref=send.at[tile, split], dst_ref=recv.at[vi, split],
             send_sem=tsend.at[tile * SPLITS + split], recv_sem=trecv.at[vi * SPLITS + split],
             device_id=(zi, tile), device_id_type=MESH,
         )
 
     def self_copy(split):
         return pltpu.make_async_copy(
-            send.at[vi, split], recv_hbm.at[vi, split], tsend.at[vi * SPLITS + split]
+            send.at[vi, split], recv.at[vi, split], tsend.at[vi * SPLITS + split]
         )
 
     def group(g):
@@ -238,7 +238,8 @@
         def mirror(step, carry):
             split = step // 8
             at = lax.rem(step, 8)
-            zs, high = lax.rem(pos["x"] + 1 + at // 2, 4), lax.rem(at, 2)
+            turn = 3 * lax.rem(at, 4) + 2 * (at // 4) + pos["y"] + 2 * pos["c"]
+            zs, high = lax.rem(pos["x"] + turn, 4), lax.rem(at // 4 + pos["c"], 2)
             tile = zs * 8 + xs * 2 + high
 
             @pl.when(split == 0)
@@ -285,8 +286,6 @@
         return carry
 
     lax.fori_loop(0, ROWS, own_row, 0)
-    out_copy = pltpu.make_async_copy(own, own_hbm, lsem.at[0])
-    out_copy.start()
     for copy in sent:
         copy.wait_send()
 
@@ -297,7 +296,7 @@
         def _():
             tile_copy(peer, split).wait_send()
             pltpu.make_async_remote_copy(
-                src_ref=send.at[peer, split], dst_ref=recv_hbm.at[peer, split],
+                src_ref=send.at[peer, split], dst_ref=recv.at[peer, split],
                 send_sem=tsend.at[step], recv_sem=trecv.at[step],
                 device_id=(zi, peer), device_id_type=MESH,
             ).wait_recv()
@@ -309,34 +308,16 @@
         return carry
 
     lax.fori_loop(0, NTILES * SPLITS, finish, 0)
-    out_copy.wait()
-
-
-def combine_kernel(back_ref, own_hbm, recv_hbm, out_hbm, own, recv, in_sem, out_sem, recv_sem):
-    load_recv = pltpu.make_async_copy(recv_hbm, recv, recv_sem)
-    load_recv.start()
-
-    def chunk(number):
-        return pl.ds(pl.multiple_of(number * CHUNK, CHUNK), CHUNK)
-
-    def load(number):
-        return pltpu.make_async_copy(
-            own_hbm.at[chunk(number)], own.at[chunk(number)], in_sem.at[number]
-        )
-
+
+
+def combine_kernel(back_ref, own, recv, out_hbm, out, out_sem):
     def store(number):
-        return pltpu.make_async_copy(
-            own.at[chunk(number)], out_hbm.at[chunk(number)], out_sem.at[number]
-        )
-
-    for number in range(ROWS // CHUNK):
-        load(number).start()
-    load_recv.wait()
+        part = pl.ds(pl.multiple_of(number * CHUNK, CHUNK), CHUNK)
+        return pltpu.make_async_copy(out.at[part], out_hbm.at[part], out_sem.at[number])
+
     low = lax.broadcasted_iota(jnp.int32, (TILE, 128), 1) < TILE
 
     def part(number, carry):
-        load(number).wait()
-
         def some_rows(some, carry):
             for r in range(4):
                 row = number * CHUNK + some * 4 + r
@@ -348,7 +329,7 @@
                     other = jnp.where(low, right, left)
                     other = jnp.concatenate([other[:, TILE:], other[:, :TILE]], axis=1)
                     stay = jnp.where(low, turns[0], turns[1]) == 0
-                    own[row, :, lanes] += jnp.where(
+                    out[row, :, lanes] = own[row, :, lanes] + jnp.where(
                         stay, kept.astype(jnp.float32), other.astype(jnp.float32)
                     )
             return carry
@@ -369,18 +350,17 @@
     own, received, back = pl.pallas_call(
         exchange_kernel,
         out_shape=(
-            jax.ShapeDtypeStruct((ROWS, TILE, KEPT * TILE), jnp.float32),
-            jax.ShapeDtypeStruct((NTILES, SPLITS, PER // 2, TILE, 2 * TILE), jnp.bfloat16),
+            pltpu.VMEM((ROWS, TILE, KEPT * TILE), jnp.float32),
+            pltpu.VMEM((NTILES, SPLITS, PER // 2, TILE, 2 * TILE), jnp.bfloat16),
             jax.ShapeDtypeStruct((2 * KEPT, ROWS), jnp.int32),
         ),
         in_specs=[vmem, vmem, anywhere],
-        out_specs=(anywhere, anywhere, vmem),
+        out_specs=(vmem, vmem, vmem),
         scratch_shapes=[
             pltpu.VMEM((4, 4, 4, 2, 16, 2048), jnp.bfloat16),
             pltpu.VMEM((2 * LANES, NTILES, TILE, 128), jnp.bfloat16),
             pltpu.VMEM((ROWS, TILE, KEPT * TILE), jnp.bfloat16),
             pltpu.VMEM((NTILES, SPLITS, PER // 2, TILE, 2 * TILE), jnp.bfloat16),
-            pltpu.VMEM((ROWS, TILE, KEPT * TILE), jnp.float32),
             pltpu.VMEM((8, NTILES * SLOTS), jnp.int32),
             pltpu.VMEM((8, ROWS), jnp.int32),
             pltpu.SMEM((8, NTILES * SLOTS), jnp.int32),
@@ -394,22 +374,19 @@
             pltpu.SemaphoreType.DMA((3,)),
         ],
         compiler_params=pltpu.CompilerParams(
-            collective_id=0, has_side_effects=True, vmem_limit_bytes=58 * 2**20
+            collective_id=0, has_side_effects=True, vmem_limit_bytes=42 * 2**20
         ),
     )(cols.transpose(0, 2, 1), fock, amps.reshape(ROWS, TILE, KEPT * TILE))
     out = pl.pallas_call(
         combine_kernel,
         out_shape=jax.ShapeDtypeStruct((ROWS, TILE, KEPT * TILE), jnp.float32),
-        in_specs=[smem, anywhere, anywhere],
+        in_specs=[smem, vmem, vmem],
         out_specs=anywhere,
         scratch_shapes=[
             pltpu.VMEM((ROWS, TILE, KEPT * TILE), jnp.float32),
-            pltpu.VMEM((NTILES * SLOTS // 2, TILE, 2 * TILE), jnp.bfloat16),
             pltpu.SemaphoreType.DMA((ROWS // CHUNK,)),
-            pltpu.SemaphoreType.DMA((ROWS // CHUNK,)),
-            pltpu.SemaphoreType.DMA,
         ],
-        compiler_params=pltpu.CompilerParams(vmem_limit_bytes=58 * 2**20),
+        compiler_params=pltpu.CompilerParams(vmem_limit_bytes=12 * 2**20),
     )(back, own, received.reshape(NTILES * SLOTS // 2, TILE, 2 * TILE))
     return out[None]
 

time: 151 us -> 142 us (0.940)
  the two profiles are of different devices: /device:TPU:15 before, /device:TPU:11 now
where the time goes in v3:
time: 142 us
  Pallas kernels  141 us (99%)
    pallas_call x1, Pallas kernels, per_device(): pl.pallas_call(exchange_kernel, out_shape=(pltpu.VMEM((ROWS, TILE, KEPT *...  136 us
    pallas_call x1, Pallas kernels, per_device(): pl.pallas_call(combine_kernel, out_shape=jax.ShapeDtypeStruct((ROWS, TILE...  5.35 us

profile of v3, /device:TPU:11, one launch (start us, length us, event | category | flops | bytes accessed | tf_op | source)
XLA Modules:
  0.0 142.0 jit_solution(11402523603739956696)
XLA Ops:
  0.0 136.0 %shard_map.37 = (f32[128,64,256]{2,1,0:T(8,128)S(1)}, bf16[32,4,4,64,128]{4,3,2,1,0:T(8,128)(2,1)S(1)}, s32[8,128]{1,0:T(8,128)}) custom-call(s32[32,4,128]{2,1,0:T(4,128)} %bitcast.6, bf16[16,2048]{1,0:T(8,128)(2,1)} %fock_ref.1, bf16[128,64,256]{2,1,0:T(8,128)(2,1)} %bitcast.5), custom_call_target="tpu_custom_call" | custom-call | tf_op jit(solution)/shard_map/pallas_call | solution.py:350
  136.0 0.0 copy-start
  136.0 0.7 copy-done
  136.7 5.3 %shard_map.38 = f32[128,64,256]{2,1,0:T(8,128)} custom-call(s32[8,128]{1,0:T(8,128)S(1)} %copy-done, f32[128,64,256]{2,1,0:T(8,128)S(1)} %get-tuple-element.9.own, bf16[512,64,128]{2,1,0:T(8,128)(2,1)S(1)} %bitcast.4), custom_call_target="tpu_custom_call" | custom-call | tf_op jit(solution)/shard_map/pallas_call | solution.py:380
Async XLA Ops:
  136.0 0.7 copy-start

commit v4 on v3

--- a/solution.py
+++ b/solution.py
@@ -74,8 +74,8 @@
 
 
 def exchange_kernel(
-    cols_ref, fock_ref, amps_hbm, own, recv, back_ref,
-    land, fa, amps, send, vtab, vown, stab, sown,
+    cols_hbm, fock_ref, amps_hbm, own, recv, back_ref,
+    land, fa, amps, send, cols_ref, vtab, vown, stab, sown,
     gsend, grecv, csend, crecv, tsend, trecv, lsem,
 ):
     zi = lax.axis_index("pairs")
@@ -84,7 +84,6 @@
     twin = {**pos, "c": 1 - pos["c"]}
 
     load_amps = pltpu.make_async_copy(amps_hbm, amps, lsem.at[0])
-    load_amps.start()
 
     barrier = pltpu.get_barrier_semaphore()
 
@@ -94,12 +93,20 @@
         )
         return carry
 
-    lax.fori_loop(1, NTILES, greet, 0)
+    for off in range(1, NTILES):
+        greet(off, 0)
     for by in (1, 2, 3):
         pl.semaphore_signal(
             barrier, inc=1, device_id=place(moved(pos, "z", by)), device_id_type=MESH
         )
-    land[pos["z"], pos["x"], pos["y"], pos["c"]] = fock_ref[...]
+    load_cols = pltpu.make_async_copy(cols_hbm, cols_ref, lsem.at[1])
+    load_cols.start()
+    load_amps.start()
+    load_rows = pltpu.make_async_copy(
+        fock_ref, land.at[pos["z"], pos["x"], pos["y"], pos["c"]], lsem.at[2]
+    )
+    load_rows.start()
+    load_rows.wait()
     pl.semaphore_wait(barrier, NTILES - 1 + 3)
 
     sent = []
@@ -115,12 +122,9 @@
             device_id=place(target), device_id_type=MESH,
         )
 
-    def push(axis, by, number, where, full="", half=None, own_rows=False):
-        dst = rows_at(where, full, half)
-        src = dst
-        if own_rows:
-            src = fock_ref if half is None else fock_ref.at[:, pl.ds(half * HALF, HALF)]
-        copy = copy_to(moved(pos, axis, by), number, src, dst)
+    def push(axis, by, number, where, full="", half=None):
+        ref = rows_at(where, full, half)
+        copy = copy_to(moved(pos, axis, by), number, ref, ref)
         copy.start()
         sent.append(copy)
 
@@ -142,13 +146,14 @@
         return moved(pos, "x", -g)
 
     def far_first(g):
-        arrived(g - 1, far(g))
-        for by in (1, 2, 3):
-            push("y", by, 15 + 6 * (g - 1) + by - 1, far(g))
+        arrived(g - 1, far(g), half=0)
+        for by in (1, 2, 3):
+            push("y", by, 15 + 6 * (g - 1) + by - 1, far(g), half=0)
 
     def far_second(g):
         for by in (1, 2, 3):
-            arrived(15 + 6 * (g - 1) + by - 1, moved(far(g), "y", -by))
+            arrived(15 + 6 * (g - 1) + by - 1, moved(far(g), "y", -by), half=0)
+        arrived(32 + g, far(g), "y", half=1)
         for by in (1, 2, 3):
             push("z", by, 18 + 6 * (g - 1) + by - 1, far(g), "y")
         across(8 + 4 * (g - 1), far(g), "y")
@@ -164,10 +169,11 @@
             came_across(8 + 4 * (g - 1) + by, moved(far(g), "z", -by), "y")
 
     for by in (1, 2, 3):
-        push("z", by, 3 + by - 1, pos, half=0, own_rows=True)
-        push("y", by, 6 + by - 1, pos, half=1, own_rows=True)
+        push("z", by, 3 + by - 1, pos, half=0)
+        push("y", by, 6 + by - 1, pos, half=1)
     for by in (1, 2, 3):
-        push("x", by, by - 1, pos, own_rows=True)
+        push("x", by, by - 1, pos, half=0)
+    load_cols.wait()
     write_tables(vi, cols_ref, vtab, vown, back_ref)
     job_table = pltpu.make_async_copy(vtab, stab, lsem.at[1])
     own_table = pltpu.make_async_copy(vown, sown, lsem.at[2])
@@ -179,6 +185,8 @@
         for by in (1, 2, 3):
             push(other, by, 9 + 3 * half + by - 1, pos, axis, half)
         across(4 * half, pos, axis, half)
+    for by in (1, 2, 3):
+        push("x", by, 32 + by, pos, "y", half=1)
     for g in (1, 2, 3):
         far_first(g)
     for by in (1, 2, 3):
@@ -354,19 +362,20 @@
             pltpu.VMEM((NTILES, SPLITS, PER // 2, TILE, 2 * TILE), jnp.bfloat16),
             jax.ShapeDtypeStruct((2 * KEPT, ROWS), jnp.int32),
         ),
-        in_specs=[vmem, vmem, anywhere],
+        in_specs=[anywhere, anywhere, anywhere],
         out_specs=(vmem, vmem, vmem),
         scratch_shapes=[
             pltpu.VMEM((4, 4, 4, 2, 16, 2048), jnp.bfloat16),
             pltpu.VMEM((2 * LANES, NTILES, TILE, 128), jnp.bfloat16),
             pltpu.VMEM((ROWS, TILE, KEPT * TILE), jnp.bfloat16),
             pltpu.VMEM((NTILES, SPLITS, PER // 2, TILE, 2 * TILE), jnp.bfloat16),
+            pltpu.VMEM((NTILES, KEPT, ROWS), jnp.int32),
             pltpu.VMEM((8, NTILES * SLOTS), jnp.int32),
             pltpu.VMEM((8, ROWS), jnp.int32),
             pltpu.SMEM((8, NTILES * SLOTS), jnp.int32),
             pltpu.SMEM((8, ROWS), jnp.int32),
-            pltpu.SemaphoreType.DMA((33,)),
-            pltpu.SemaphoreType.DMA((33,)),
+            pltpu.SemaphoreType.DMA((36,)),
+            pltpu.SemaphoreType.DMA((36,)),
             pltpu.SemaphoreType.DMA((20,)),
             pltpu.SemaphoreType.DMA((20,)),
             pltpu.SemaphoreType.DMA((NTILES * SPLITS,)),

time: 142 us -> 136 us (0.958)
  the two profiles are of different devices: /device:TPU:11 before, /device:TPU:1 now
where the time goes in v4:
time: 136 us
  Pallas kernels  135 us (99%)
    pallas_call x1, Pallas kernels, per_device(): pl.pallas_call(exchange_kernel, out_shape=(pltpu.VMEM((ROWS, TILE, KEPT *...  130 us
    pallas_call x1, Pallas kernels, per_device(): pl.pallas_call(combine_kernel, out_shape=jax.ShapeDtypeStruct((ROWS, TILE...  5.35 us

profile of v4, /device:TPU:1, one launch (start us, length us, event | category | flops | bytes accessed | tf_op | source)
XLA Modules:
  0.0 135.6 jit_solution(4660211567690574798)
XLA Ops:
  0.0 129.6 %shard_map.37 = (f32[128,64,256]{2,1,0:T(8,128)S(1)}, bf16[32,4,4,64,128]{4,3,2,1,0:T(8,128)(2,1)S(1)}, s32[8,128]{1,0:T(8,128)}) custom-call(s32[32,4,128]{2,1,0:T(4,128)} %bitcast.6, bf16[16,2048]{1,0:T(8,128)(2,1)} %fock_ref.1, bf16[128,64,256]{2,1,0:T(8,128)(2,1)} %bitcast.5), custom_call_target="tpu_custom_call" | custom-call | tf_op jit(solution)/shard_map/pallas_call | solution.py:358
  129.6 0.0 copy-start
  129.6 0.7 copy-done
  130.3 5.3 %shard_map.38 = f32[128,64,256]{2,1,0:T(8,128)} custom-call(s32[8,128]{1,0:T(8,128)S(1)} %copy-done, f32[128,64,256]{2,1,0:T(8,128)S(1)} %get-tuple-element.9.own, bf16[512,64,128]{2,1,0:T(8,128)(2,1)S(1)} %bitcast.4), custom_call_target="tpu_custom_call" | custom-call | tf_op jit(solution)/shard_map/pallas_call | solution.py:389
Async XLA Ops:
  129.6 0.7 copy-start

commit v5 on v4

--- a/solution.py
+++ b/solution.py
@@ -17,7 +17,7 @@
 SLOTS = 32
 PER = SLOTS // SPLITS
 LANES = 16
-CHUNK = 16
+CHUNK = 8
 HALF = 1024
 
 
@@ -246,7 +246,7 @@
         def mirror(step, carry):
             split = step // 8
             at = lax.rem(step, 8)
-            turn = 3 * lax.rem(at, 4) + 2 * (at // 4) + pos["y"] + 2 * pos["c"]
+            turn = lax.rem(at, 4) + 2 * (at // 4) + pos["y"] + 2 * pos["c"] + 3 * split + 1
             zs, high = lax.rem(pos["x"] + turn, 4), lax.rem(at // 4 + pos["c"], 2)
             tile = zs * 8 + xs * 2 + high
 
@@ -298,20 +298,25 @@
         copy.wait_send()
 
     def finish(step, carry):
-        peer, split = step // SPLITS, lax.rem(step, SPLITS)
+        g, split, at = step // (8 * SPLITS), lax.rem(step // 8, SPLITS), lax.rem(step, 8)
+        tile = (at // 2) * 8 + lax.rem(pos["x"] + 4 - g, 4) * 2 + lax.rem(at, 2)
+        peer = lax.rem(pos["y"] + g, 4) * 8 + at
+
+        @pl.when(tile != vi)
+        def _():
+            tile_copy(tile, split).wait_send()
+
+        @pl.when(tile == vi)
+        def _():
+            self_copy(split).wait()
 
         @pl.when(peer != vi)
         def _():
-            tile_copy(peer, split).wait_send()
             pltpu.make_async_remote_copy(
                 src_ref=send.at[peer, split], dst_ref=recv.at[peer, split],
-                send_sem=tsend.at[step], recv_sem=trecv.at[step],
+                send_sem=tsend.at[peer * SPLITS + split], recv_sem=trecv.at[peer * SPLITS + split],
                 device_id=(zi, peer), device_id_type=MESH,
             ).wait_recv()
-
-        @pl.when(peer == vi)
-        def _():
-            self_copy(split).wait()
 
         return carry
 

time: 136 us -> 134 us (0.985)
  Pallas kernels: 135 us -> 133 us
    pallas_call x1, Pallas kernels: 130 us -> 128 us  [per_device(): pl.pallas_call(exchange_kernel, out_shape=(pltpu.VMEM((ROWS, TILE, KEPT *...]
where the time goes in v5:
time: 134 us
  Pallas kernels  133 us (99%)
    pallas_call x1, Pallas kernels, per_device(): pl.pallas_call(exchange_kernel, out_shape=(pltpu.VMEM((ROWS, TILE, KEPT *...  128 us
    pallas_call x1, Pallas kernels, per_device(): pl.pallas_call(combine_kernel, out_shape=jax.ShapeDtypeStruct((ROWS, TILE...  5.28 us

profile of v5, /device:TPU:1, one launch (start us, length us, event | category | flops | bytes accessed | tf_op | source)
XLA Modules:
  0.0 133.9 jit_solution(8727970565739372295)
XLA Ops:
  0.0 128.0 %shard_map.37 = (f32[128,64,256]{2,1,0:T(8,128)S(1)}, bf16[32,4,4,64,128]{4,3,2,1,0:T(8,128)(2,1)S(1)}, s32[8,128]{1,0:T(8,128)}) custom-call(s32[32,4,128]{2,1,0:T(4,128)} %bitcast.6, bf16[16,2048]{1,0:T(8,128)(2,1)} %fock_ref.1, bf16[128,64,256]{2,1,0:T(8,128)(2,1)} %bitcast.5), custom_call_target="tpu_custom_call" | custom-call | tf_op jit(solution)/shard_map/pallas_call | solution.py:363
  128.0 0.0 copy-start
  128.0 0.7 copy-done
  128.6 5.3 %shard_map.38 = f32[128,64,256]{2,1,0:T(8,128)} custom-call(s32[8,128]{1,0:T(8,128)S(1)} %copy-done, f32[128,64,256]{2,1,0:T(8,128)S(1)} %get-tuple-element.9.own, bf16[512,64,128]{2,1,0:T(8,128)(2,1)S(1)} %bitcast.4), custom_call_target="tpu_custom_call" | custom-call | tf_op jit(solution)/shard_map/pallas_call | solution.py:394
Async XLA Ops:
  128.0 0.7 copy-start

commit v6 on v5

--- a/solution.py
+++ b/solution.py
@@ -332,8 +332,8 @@
 
     def part(number, carry):
         def some_rows(some, carry):
-            for r in range(4):
-                row = number * CHUNK + some * 4 + r
+            for r in range(8):
+                row = number * CHUNK + some * 8 + r
                 for h in range(2):
                     lanes = pl.ds(h * 128, 128)
                     left, right = [recv[back_ref[2 * h + i, row]] for i in range(2)]
@@ -347,7 +347,7 @@
                     )
             return carry
 
-        lax.fori_loop(0, CHUNK // 4, some_rows, 0)
+        lax.fori_loop(0, CHUNK // 8, some_rows, 0)
         store(number).start()
         return carry
 

time: 134 us -> 133 us (level)
  no operation moved by 1% of the time
where the time goes in v6:
time: 133 us
  Pallas kernels  132 us (99%)
    pallas_call x1, Pallas kernels, per_device(): pl.pallas_call(exchange_kernel, out_shape=(pltpu.VMEM((ROWS, TILE, KEPT *...  128 us
    pallas_call x1, Pallas kernels, per_device(): pl.pallas_call(combine_kernel, out_shape=jax.ShapeDtypeStruct((ROWS, TILE...  4.33 us

profile of v6, /device:TPU:1, one launch (start us, length us, event | category | flops | bytes accessed | tf_op | source)
XLA Modules:
  0.0 133.0 jit_solution(3704209938967043692)
XLA Ops:
  0.0 128.0 %shard_map.37 = (f32[128,64,256]{2,1,0:T(8,128)S(1)}, bf16[32,4,4,64,128]{4,3,2,1,0:T(8,128)(2,1)S(1)}, s32[8,128]{1,0:T(8,128)}) custom-call(s32[32,4,128]{2,1,0:T(4,128)} %bitcast.6, bf16[16,2048]{1,0:T(8,128)(2,1)} %fock_ref.1, bf16[128,64,256]{2,1,0:T(8,128)(2,1)} %bitcast.5), custom_call_target="tpu_custom_call" | custom-call | tf_op jit(solution)/shard_map/pallas_call | solution.py:363
  128.0 0.0 copy-start
  128.0 0.7 copy-done
  128.6 4.3 %shard_map.38 = f32[128,64,256]{2,1,0:T(8,128)} custom-call(s32[8,128]{1,0:T(8,128)S(1)} %copy-done, f32[128,64,256]{2,1,0:T(8,128)S(1)} %get-tuple-element.9.own, bf16[512,64,128]{2,1,0:T(8,128)(2,1)S(1)} %bitcast.4), custom_call_target="tpu_custom_call" | custom-call | tf_op jit(solution)/shard_map/pallas_call | solution.py:394
Async XLA Ops:
  128.0 0.7 copy-start
